TPU v7x, 256 devices: a whole 4x4x8 slice. The times are simulated.
256 devices in a mesh: shot: 64 (over z, x_lo, y), rcv: 4 (over x_hi, core).
Axes of the slice: x: 4 (x_hi: 2, x_lo: 2; x = x_hi * 2 + x_lo), y: 4, z: 8, core: 2. Of those that a mesh axis runs over, the one named last changes fastest.
Arguments:
- records: bfloat16 [1, 2, 8192, 8192], P(None, None, 'shot', 'rcv'), may hold values from -6 to 6
- aperture: int32 [8192, 2], P('shot'), may hold values from 0 to 3, all different within a row
- block_owner: int32 [4], replicated, may hold values from 0 to 63, as said below
- block_receivers: int32 [4, 128], replicated, may hold values from 0 to 8191, as said below
Outputs:
- multiples: bfloat16 [1, 2, 8192, 8192], P(None, None, 'shot', 'rcv')
Inputs may be any that keep to these rules, and one draw needn't show every extreme that they name: `block_owner`: distinct indices. `block_receivers`: distinct receivers.
All inputs are finite; a program needn't handle non-finite values.
Results may differ from a plain program's by a relative error of at most 0.001.
Values may be sent and summed in bfloat16 or wider, within the bound.
A program may use at most 128 MiB of HBM per device.

v0:
```python
import functools

import jax
import jax.numpy as jnp
from jax import lax
from jax.experimental import pallas as pl
from jax.experimental.pallas import tpu as pltpu
from jax.sharding import PartitionSpec as P

MESH = pl.DeviceIdType.MESH
BF16 = jnp.bfloat16
APER = 2
BLOCK = 128
NBLK = 4
NX, NY, NZ, NR = 2, 4, 8, 4
NQ = NX * NY
SHARE = 256
NC = 2
LANES = SHARE // NC
ROWS = 2 * BLOCK
SUB = ROWS // NZ


def remote(src, dst, send_sem, recv_sem, device):
    return pltpu.make_async_remote_copy(
        src_ref=src, dst_ref=dst, send_sem=send_sem, recv_sem=recv_sem, device_id=device, device_id_type=MESH
    )


def kernel(
    rec, aperture, owner, receivers, out,
    scat0, scat1, zscat0, zscat1, sel, part, gath, far, near, local, given, stage,
    s1s, s1r, s2s, s2r, s3s, s3r, n1s, n1r, n2s, n2r, n3s, n3r, os, orr,
):
    scat, zscat = (scat0, scat1), (zscat0, zscat1)
    shot, r = lax.axis_index("shot"), lax.axis_index("rcv")
    z, q = shot // NQ, lax.rem(shot, NQ)
    core = lax.rem(r, 2)
    other_core = (shot, r + 1 - 2 * core)
    other_x = (shot, lax.rem(r + 2, NR))

    def plane(d):
        index = lax.rem(q + d, NQ)
        return index, (z * NQ + index, r)

    def line(d):
        index = lax.rem(z + d, NZ)
        return index, (index * NQ + q, r)

    barrier = pltpu.get_barrier_semaphore()
    for d in range(1, NQ):
        pl.semaphore_signal(barrier, inc=1, device_id=plane(d)[1], device_id_type=MESH)
    for d in range(1, NZ):
        pl.semaphore_signal(barrier, inc=1, device_id=line(d)[1], device_id_type=MESH)
    pl.semaphore_signal(barrier, inc=1, device_id=other_core, device_id_type=MESH)
    pl.semaphore_signal(barrier, inc=1, device_id=other_x, device_id_type=MESH)
    pl.semaphore_wait(barrier, NQ - 1 + NZ - 1 + 2)

    def columns(index, n):
        return pl.ds(pl.multiple_of(index * SHARE + n * LANES, LANES), LANES)

    def s1(n, d, source):
        index, device = plane(d)
        return remote(
            rec.at[:, columns(index, n)], scat[n].at[source], s1s.at[n, d], s1r.at[n, source], device
        )

    def s2(n, d, source):
        index, device = line(d)
        return remote(sel.at[n, index], zscat[n].at[source], s2s.at[n, d], s2r.at[n, source], device)

    def s3(n, d, source):
        index, device = line(d)
        return remote(part.at[n], gath.at[n, source], s3s.at[n, d], s3r.at[n, source], device)

    def o(n, d, source):
        index, device = plane(d)
        return remote(
            stage.at[n, index], out.at[:, columns(source, n)], os.at[n, d], orr.at[n, source], device
        )

    def n2(d, source):
        index, device = plane(d)
        return remote(
            near.at[q, core], near.at[source, core], n2s.at[d], n2r.at[source], device
        )

    def n3(index, half):
        return remote(near.at[index, half], near.at[index, half], n3s.at[index], n3r.at[index], other_core)

    for n in range(NC):
        for d in range(1, NQ):
            s1(n, d, q).start()
    for n in range(NC):
        scat[n][q] = rec[:, columns(q, n)]

    first = r * (NQ * SHARE)
    points = jnp.concatenate([receivers[b : b + 1, :] for b in range(NBLK)], axis=1)
    tile = 256
    total = jnp.zeros((ROWS, NBLK * BLOCK), jnp.float32)
    for k in range(NQ * SHARE // tile):
        ids = first + k * tile + lax.broadcasted_iota(jnp.int32, (tile, NBLK * BLOCK), 0)
        chosen = jnp.where(ids == points, 1.0, 0.0).astype(BF16)
        total += jnp.dot(rec[:, k * tile : (k + 1) * tile], chosen, preferred_element_type=jnp.float32)
    block = lax.broadcasted_iota(jnp.int32, (BLOCK, NBLK * BLOCK), 1) // BLOCK
    use = (block == aperture[:, 0:1]) | (block == aperture[:, 1:2])
    for c in range(2):
        local[c] = jnp.where(use, total[c * BLOCK : (c + 1) * BLOCK], 0.0).astype(BF16)

    n1a = remote(local.at[1 - core], given.at[0], n1s.at[0], n1r.at[0], other_core)
    n1a.start()
    n1a.wait_recv()
    given[2] = local[core] + given[0]
    n1b = remote(given.at[2], given.at[1], n1s.at[1], n1r.at[1], other_x)
    n1b.start()

    zb = [owner[b] // NQ for b in range(NBLK)]
    qb = [lax.rem(owner[b], NQ) for b in range(NBLK)]

    def to_line(n):
        for d in range(1, NQ):
            source = lax.rem(q + d, NQ)
            s1(n, d, source).wait_recv()
        for b in range(NBLK):
            piece = scat[n][qb[b]]
            for k in range(NZ):
                sel[n, k, b] = piece[k * SUB : (k + 1) * SUB]
        for d in range(1, NZ):
            s2(n, d, z).start()
        zscat[n][z] = sel[n, z]

    def gather_line(n):
        for d in range(1, NZ):
            s2(n, d, lax.rem(z + d, NZ)).wait_recv()
        for b in range(NBLK):
            part[n, b] = zscat[n][zb[b], b]
        for d in range(1, NZ):
            s3(n, d, z).start()
        gath[n, z] = part[n]

    to_line(0)
    n1b.wait_recv()
    near[q, core] = given[1] + given[2]
    for d in range(1, NQ):
        n2(d, q).start()
    n3(q, core).start()
    to_line(1)
    gather_line(0)
    gather_line(1)
    for d in range(1, NQ):
        source = lax.rem(q + d, NQ)
        n2(d, source).wait_recv()
        n3(source, core).start()
    for d in range(NQ):
        n3(lax.rem(q + d, NQ), 1 - core).wait_recv()

    factor = (2.0 * APER * BLOCK) ** (-0.5)
    half = NZ // 2
    for n in range(NC):
        for d in range(1, NZ):
            s3(n, d, lax.rem(z + d, NZ)).wait_recv()
        for k in range(NZ):
            for b in range(NBLK):
                start = b * BLOCK + (k % half) * SUB
                far[n, k // half, start : start + SUB] = gath[n, k, b]

        def product(index):
            rows = near[index].reshape(ROWS, NBLK * BLOCK)
            by_real = jnp.dot(rows, far[n, 0], preferred_element_type=jnp.float32)
            by_imag = jnp.dot(rows, far[n, 1], preferred_element_type=jnp.float32)
            real = by_real[:BLOCK] - by_imag[BLOCK:]
            imag = by_real[BLOCK:] + by_imag[:BLOCK]
            return (jnp.concatenate([real, imag], axis=0) * factor).astype(BF16)

        for d in range(1, NQ):
            index = lax.rem(q + d, NQ)
            stage[n, index] = product(index)
            o(n, d, q).start()
        out[:, columns(q, n)] = product(q)

    for n in range(NC):
        for d in range(1, NQ):
            o(n, d, lax.rem(q + d, NQ)).wait_recv()
    n1a.wait_send()
    n1b.wait_send()
    for d in range(1, NQ):
        n2(d, q).wait_send()
    for index in range(NQ):
        n3(index, core).wait_send()
    for n in range(NC):
        for d in range(1, NQ):
            s1(n, d, q).wait_send()
            o(n, d, q).wait_send()
        for d in range(1, NZ):
            s2(n, d, z).wait_send()
            s3(n, d, z).wait_send()


def per_device(records, aperture, block_owner, block_receivers):
    freqs, parts, shots_here, rcv_here = records.shape
    vmem = pl.BlockSpec(memory_space=pltpu.VMEM)
    dma = pltpu.SemaphoreType.DMA
    out = pl.pallas_call(
        kernel,
        out_shape=jax.ShapeDtypeStruct((ROWS, rcv_here), BF16),
        in_specs=[vmem, vmem, pl.BlockSpec(memory_space=pltpu.SMEM), vmem],
        out_specs=vmem,
        scratch_shapes=[
            pltpu.VMEM((NQ, ROWS, LANES), BF16),
            pltpu.VMEM((NQ, ROWS, LANES), BF16),
            pltpu.VMEM((NZ, NBLK, SUB, LANES), BF16),
            pltpu.VMEM((NZ, NBLK, SUB, LANES), BF16),
            pltpu.VMEM((NC, NZ, NBLK, SUB, LANES), BF16),
            pltpu.VMEM((NC, NBLK, SUB, LANES), BF16),
            pltpu.VMEM((NC, NZ, NBLK, SUB, LANES), BF16),
            pltpu.VMEM((NC, 2, NBLK * BLOCK, LANES), BF16),
            pltpu.VMEM((NQ, 2, BLOCK, NBLK * BLOCK), BF16),
            pltpu.VMEM((2, BLOCK, NBLK * BLOCK), BF16),
            pltpu.VMEM((3, BLOCK, NBLK * BLOCK), BF16),
            pltpu.VMEM((NC, NQ, ROWS, LANES), BF16),
            dma((NC, NQ)), dma((NC, NQ)),
            dma((NC, NZ)), dma((NC, NZ)),
            dma((NC, NZ)), dma((NC, NZ)),
            dma((2,)), dma((2,)),
            dma((NQ,)), dma((NQ,)),
            dma((NQ,)), dma((NQ,)),
            dma((NC, NQ)), dma((NC, NQ)),
        ],
        compiler_params=pltpu.CompilerParams(
            collective_id=0, has_side_effects=True, vmem_limit_bytes=48 * 1024 * 1024
        ),
        cost_estimate=pl.CostEstimate(flops=2 * 10**9, bytes_accessed=2 * 2**20, transcendentals=0),
    )(records.reshape(ROWS, rcv_here), aperture, block_owner, block_receivers)
    return out.reshape(freqs, parts, shots_here, rcv_here)


def solution(mesh):
    placed = (P(None, None, "shot", "rcv"), P("shot", None), P(), P())
    return jax.shard_map(
        per_device,
        mesh=mesh,
        in_specs=placed,
        out_specs=P(None, None, "shot", "rcv"),
        check_vma=False,
    )
```

profile of v0, /device:TPU:1, one launch (start us, length us, event | category | flops | bytes accessed | tf_op | source)
XLA Modules:
  0.0 62.2 jit_solution(8645338329840270096)
XLA Ops:
  0.0 0.0 copy-start.3
  0.0 0.7 %copy-done.3 = s32[128,2]{0,1:T(2,128)S(1)} copy-done((s32[128,2]{0,1:T(2,128)S(1)}, s32[128,2]{0,1:T(2,128)}, u32[]{:S(2)}) %copy-start.3) | copy-done | bytes 1048
  0.7 0.0 copy-start.1
  0.7 0.0 copy-start.2
  0.7 0.1 copy.5.aperture
  0.8 0.6 copy-done.1
  1.4 0.0 copy-done.2
  1.4 0.0 copy-start
  1.4 1.2 %copy-done = bf16[1,2,128,2048]{3,2,1,0:T(8,128)(2,1)S(1)} copy-done((bf16[1,2,128,2048]{3,2,1,0:T(8,128)(2,1)S(1)}, bf16[1,2,128,2048]{3,2,1,0:T(8,128)(2,1)}, u32[]{:S(2)}) %copy-start) | copy-done | bytes 1048600
  2.6 58.7 %shard_map.46 = bf16[256,2048]{1,0:T(8,128)(2,1)S(1)} custom-call(bf16[256,2048]{1,0:T(8,128)(2,1)S(1)} %bitcast.3, s32[128,2]{1,0:T(8,128)S(1)} %copy.5.aperture, s32[4]{0:T(128)S(1)} %copy-done.2, s32[4,128]{1,0:T(4,128)S(1)} %copy-done.1), custom_call_target="tpu_custom_call" | custom-call | flops 2000000000 | bytes 2097152 | tf_op jit(solution)/shard_map/pallas_call | solution.py:203
  61.3 1.0 %copy.7 = bf16[1,2,128,2048]{3,2,1,0:T(8,128)(2,1)} copy(bf16[1,2,128,2048]{3,2,1,0:T(8,128)(2,1)S(1)} %bitcast.2) | data formatting | bytes 2097152
Async XLA Ops:
  0.0 0.7 %copy-start.3 = (s32[128,2]{0,1:T(2,128)S(1)}, s32[128,2]{0,1:T(2,128)}, u32[]{:S(2)}) copy-start(s32[128,2]{0,1:T(2,128)} %param.5) | copy-start | bytes 3076
  0.7 0.7 %copy-start.1 = (s32[4,128]{1,0:T(4,128)S(1)}, s32[4,128]{1,0:T(4,128)}, u32[]{:S(2)}) copy-start(s32[4,128]{1,0:T(4,128)} %receivers.1) | copy-start | bytes 6148
  0.7 0.7 %copy-start.2 = (s32[4]{0:T(128)S(1)}, s32[4]{0:T(128)}, u32[]{:S(2)}) copy-start(s32[4]{0:T(128)} %owner.1) | copy-start | bytes 52
  1.4 1.2 %copy-start = (bf16[1,2,128,2048]{3,2,1,0:T(8,128)(2,1)S(1)}, bf16[1,2,128,2048]{3,2,1,0:T(8,128)(2,1)}, u32[]{:S(2)}) copy-start(bf16[1,2,128,2048]{3,2,1,0:T(8,128)(2,1)} %param.4) | copy-start | bytes 3145732
where the time goes:
time: 62.4 us; the launch traced here: 62.2 us
  Pallas kernels  58.7 us (94%)
  local copies, waits for them, and re-layouts  3.56 us (6%)
    pallas_call x1, Pallas kernels, per_device(): pl.pallas_call(kernel, out_shape=jax.ShapeDtypeStruct((ROWS, rcv_here), B...  58.7 us
    unnamed x10, local copies, waits for them, and re-layouts  3.56 us

commit v1 on v0

v1 whole, which is shorter than its diff:
```python
import jax
import jax.numpy as jnp
from jax import lax
from jax.experimental import pallas as pl
from jax.experimental.pallas import tpu as pltpu
from jax.sharding import PartitionSpec as P

MESH = pl.DeviceIdType.MESH
BF16 = jnp.bfloat16
F32 = jnp.float32
APER = 2
BLOCK = 128
NBLK = 4
NX, NY, NZ, NR = 2, 4, 8, 4
NQ = NX * NY
SHARE = 256
NC = 2
LANES = SHARE // NC
ROWS = 2 * BLOCK
SUB = BLOCK // NZ
WIDTH = APER * BLOCK
TAIL = 16
SHIFT = (1, NZ - 1)


def remote(src, dst, send_sem, recv_sem, device):
    return pltpu.make_async_remote_copy(
        src_ref=src, dst_ref=dst, send_sem=send_sem, recv_sem=recv_sem, device_id=device, device_id_type=MESH
    )


def kernel(
    rec_hbm, ap_hbm, owner_hbm, recv_hbm, out,
    rec, ap, receivers, owner,
    scat0, scat1, zscat0, zscat1, sel, part, gath, far, near, local, given, lhs, stage,
    ins, s1s, s1r, s2s, s2r, s3s, s3r, n1s, n1r, n2s, n2r, n3s, n3r, os, orr,
):
    scat, zscat = (scat0, scat1), (zscat0, zscat1)
    shot, r = lax.axis_index("shot"), lax.axis_index("rcv")
    z, q = shot // NQ, lax.rem(shot, NQ)
    core = lax.rem(r, 2)
    other_core = (shot, r + 1 - 2 * core)
    other_x = (shot, lax.rem(r + 2, NR))

    inputs = [
        pltpu.make_async_copy(src, dst, ins.at[k])
        for k, (src, dst) in enumerate(((rec_hbm, rec), (ap_hbm, ap), (recv_hbm, receivers), (owner_hbm, owner)))
    ]
    for copy in inputs:
        copy.start()

    def at(index, plane):
        return (plane * NQ + index, r)

    def plane(d):
        index = lax.rem(q + d, NQ)
        return index, at(index, z)

    def line(d):
        index = lax.rem(z + d, NZ)
        return index, at(q, index)

    barrier = pltpu.get_barrier_semaphore()
    for d in range(1, NQ):
        index = lax.rem(q + d, NQ)
        for plane_of in (z, *(lax.rem(z + shift, NZ) for shift in SHIFT)):
            pl.semaphore_signal(barrier, inc=1, device_id=at(index, plane_of), device_id_type=MESH)
    for d in range(1, NZ):
        pl.semaphore_signal(barrier, inc=1, device_id=line(d)[1], device_id_type=MESH)
    pl.semaphore_signal(barrier, inc=1, device_id=other_core, device_id_type=MESH)
    pl.semaphore_signal(barrier, inc=1, device_id=other_x, device_id_type=MESH)
    pl.semaphore_wait(barrier, 3 * (NQ - 1) + NZ - 1 + 2)

    def columns(index, n):
        return pl.ds(pl.multiple_of(index * SHARE + n * LANES, LANES), LANES)

    def s1(n, e, d, source):
        index = lax.rem(q + d, NQ)
        return remote(
            rec_hbm.at[pl.ds(e * BLOCK, BLOCK), columns(index, n)], scat[n].at[e, source],
            s1s.at[n, e, d], s1r.at[n, e, source], at(index, lax.rem(z + e * SHIFT[n], NZ)),
        )

    def s2(n, d, source):
        index, device = line(d)
        return remote(sel.at[n, index], zscat[n].at[source], s2s.at[n, d], s2r.at[n, source], device)

    def s3(n, d, source):
        return remote(part.at[n], gath.at[n, source], s3s.at[n, d], s3r.at[n, source], line(d)[1])

    def o(n, d, source):
        index, device = plane(d)
        return remote(stage.at[n, index], out.at[:, columns(source, n)], os.at[n, d], orr.at[n, source], device)

    def n2(d, source):
        return remote(near.at[q, core], near.at[source, core], n2s.at[d], n2r.at[source], plane(d)[1])

    def n3(index, half):
        return remote(near.at[index, half], near.at[index, half], n3s.at[index], n3r.at[index], other_core)

    offsets = [[(e, d) for d in range(NQ) for e in (1, 0) if (e, d) != (0, 0)]] * NC
    for n in range(NC):
        for e, d in offsets[n]:
            s1(n, e, d, q).start()
    for copy in inputs:
        copy.wait()
    for n in range(NC):
        scat[n][0, q] = rec[:BLOCK, columns(q, n)]

    first = r * (NQ * SHARE)
    points = jnp.concatenate([receivers[b : b + 1, :] for b in range(NBLK)], axis=1)
    tile = 256
    total = jnp.zeros((ROWS, NBLK * BLOCK), F32)
    for k in range(NQ * SHARE // tile):
        ids = first + k * tile + lax.broadcasted_iota(jnp.int32, (tile, NBLK * BLOCK), 0)
        chosen = jnp.where(ids == points, 1.0, 0.0).astype(BF16)
        total += jnp.dot(rec[:, k * tile : (k + 1) * tile], chosen, preferred_element_type=F32)
    diagonal = lax.broadcasted_iota(jnp.int32, (BLOCK, BLOCK), 0) == lax.broadcasted_iota(
        jnp.int32, (BLOCK, BLOCK), 1
    )

    def upright(row):
        return jnp.sum(jnp.where(diagonal, row, 0.0), axis=1, keepdims=True)

    apertures = ap[...].astype(F32)
    for a in range(APER):
        block = upright(apertures[a : a + 1])
        for c in range(2):
            rows = total[c * BLOCK : (c + 1) * BLOCK]
            found = rows[:, :BLOCK]
            for b in range(1, NBLK):
                found = jnp.where(block == b, rows[:, b * BLOCK : (b + 1) * BLOCK], found)
            local[c, :, a * BLOCK : (a + 1) * BLOCK] = found.astype(BF16)

    n1a = remote(local.at[1 - core], given.at[0], n1s.at[0], n1r.at[0], other_core)
    n1a.start()
    tail = jnp.concatenate([apertures[a : a + 1] for a in range(APER)], axis=1)
    near[q, core, BLOCK:] = jnp.broadcast_to(tail, (TAIL, WIDTH)).astype(BF16)
    n1a.wait_recv()
    given[2] = local[core] + given[0]
    n1b = remote(given.at[2], given.at[1], n1s.at[1], n1r.at[1], other_x)
    n1b.start()

    zb = [owner[b] // NQ for b in range(NBLK)]
    qb = [lax.rem(owner[b], NQ) for b in range(NBLK)]

    def to_line(n):
        for e, d in offsets[n]:
            s1(n, e, d, lax.rem(q + d, NQ)).wait_recv()
        for b in range(NBLK):
            piece = scat[n][jnp.where(zb[b] == z, 0, 1), qb[b]]
            for k in range(NZ):
                sel[n, k, b] = piece[k * SUB : (k + 1) * SUB]
        for d in range(1, NZ):
            s2(n, d, z).start()
        zscat[n][z] = sel[n, z]

    def gather_line(n):
        for d in range(1, NZ):
            s2(n, d, lax.rem(z + d, NZ)).wait_recv()
        for b in range(NBLK):
            for c in range(2):
                part[n, b, c] = zscat[n][lax.rem(zb[b] + c * SHIFT[n], NZ), b]
        for d in range(1, NZ):
            s3(n, d, z).start()
        gath[n, z] = part[n]

    to_line(0)
    n1b.wait_recv()
    near[q, core, :BLOCK] = given[1] + given[2]
    for d in range(1, NQ):
        n2(d, q).start()
    n3(q, core).start()
    to_line(1)
    gather_line(0)
    gather_line(1)
    for d in range(1, NQ):
        source = lax.rem(q + d, NQ)
        n2(d, source).wait_recv()
        n3(source, core).start()
    for d in range(NQ):
        index = lax.rem(q + d, NQ)
        n3(index, 1 - core).wait_recv()
        tail = near[index, 0, BLOCK:].astype(F32)
        blocks = [upright(tail[:1, a * BLOCK : (a + 1) * BLOCK]) for a in range(APER)]
        for b in range(NBLK):
            use = [(block == b).astype(F32).astype(BF16) for block in blocks]
            for c in range(2):
                lhs[index, c, :, b * BLOCK : (b + 1) * BLOCK] = (
                    near[index, c, :BLOCK, :BLOCK] * use[0] + near[index, c, :BLOCK, BLOCK:] * use[1]
                )

    factor = (2.0 * APER * BLOCK) ** (-0.5)
    for n in range(NC):
        for d in range(1, NZ):
            s3(n, d, lax.rem(z + d, NZ)).wait_recv()
        for k in range(NZ):
            for b in range(NBLK):
                for c in range(2):
                    far[n, c, b * BLOCK + k * SUB : b * BLOCK + (k + 1) * SUB] = gath[n, k, b, c]

        def product(index):
            rows = lhs[index].reshape(ROWS, NBLK * BLOCK)
            by_real = jnp.dot(rows, far[n, 0], preferred_element_type=F32)
            by_imag = jnp.dot(rows, far[n, 1], preferred_element_type=F32)
            real = by_real[:BLOCK] - by_imag[BLOCK:]
            imag = by_real[BLOCK:] + by_imag[:BLOCK]
            return (jnp.concatenate([real, imag], axis=0) * factor).astype(BF16)

        for d in range(1, NQ):
            index = lax.rem(q + d, NQ)
            stage[n, index] = product(index)
            o(n, d, q).start()
        out[:, columns(q, n)] = product(q)

    for n in range(NC):
        for d in range(1, NQ):
            o(n, d, lax.rem(q + d, NQ)).wait_recv()
    n1a.wait_send()
    n1b.wait_send()
    for d in range(1, NQ):
        n2(d, q).wait_send()
    for index in range(NQ):
        n3(index, core).wait_send()
    for n in range(NC):
        for e, d in offsets[n]:
            s1(n, e, d, q).wait_send()
        for d in range(1, NQ):
            o(n, d, q).wait_send()
        for d in range(1, NZ):
            s2(n, d, z).wait_send()
            s3(n, d, z).wait_send()


def per_device(records, aperture, block_owner, block_receivers):
    freqs, parts, shots_here, rcv_here = records.shape
    hbm = pl.BlockSpec(memory_space=pltpu.HBM)
    dma = pltpu.SemaphoreType.DMA
    out = pl.pallas_call(
        kernel,
        out_shape=jax.ShapeDtypeStruct((ROWS, rcv_here), BF16),
        in_specs=[hbm] * 4,
        out_specs=pl.BlockSpec(memory_space=pltpu.VMEM),
        scratch_shapes=[
            pltpu.VMEM((ROWS, NQ * SHARE), BF16),
            pltpu.VMEM((APER, BLOCK), jnp.int32),
            pltpu.VMEM((NBLK, BLOCK), jnp.int32),
            pltpu.SMEM((NBLK,), jnp.int32),
            pltpu.VMEM((2, NQ, BLOCK, LANES), BF16),
            pltpu.VMEM((2, NQ, BLOCK, LANES), BF16),
            pltpu.VMEM((NZ, NBLK, SUB, LANES), BF16),
            pltpu.VMEM((NZ, NBLK, SUB, LANES), BF16),
            pltpu.VMEM((NC, NZ, NBLK, SUB, LANES), BF16),
            pltpu.VMEM((NC, NBLK, 2, SUB, LANES), BF16),
            pltpu.VMEM((NC, NZ, NBLK, 2, SUB, LANES), BF16),
            pltpu.VMEM((NC, 2, NBLK * BLOCK, LANES), BF16),
            pltpu.VMEM((NQ, 2, BLOCK + TAIL, WIDTH), BF16),
            pltpu.VMEM((2, BLOCK, WIDTH), BF16),
            pltpu.VMEM((3, BLOCK, WIDTH), BF16),
            pltpu.VMEM((NQ, 2, BLOCK, NBLK * BLOCK), BF16),
            pltpu.VMEM((NC, NQ, ROWS, LANES), BF16),
            dma((4,)),
            dma((NC, 2, NQ)), dma((NC, 2, NQ)),
            dma((NC, NZ)), dma((NC, NZ)),
            dma((NC, NZ)), dma((NC, NZ)),
            dma((2,)), dma((2,)),
            dma((NQ,)), dma((NQ,)),
            dma((NQ,)), dma((NQ,)),
            dma((NC, NQ)), dma((NC, NQ)),
        ],
        compiler_params=pltpu.CompilerParams(
            collective_id=0, has_side_effects=True, vmem_limit_bytes=56 * 1024 * 1024
        ),
        cost_estimate=pl.CostEstimate(flops=2 * 10**9, bytes_accessed=2 * 2**20, transcendentals=0),
    )(records.reshape(ROWS, rcv_here), aperture.T, block_owner, block_receivers)
    return out.reshape(freqs, parts, shots_here, rcv_here)


def solution(mesh):
    placed = (P(None, None, "shot", "rcv"), P("shot", None), P(), P())
    return jax.shard_map(
        per_device,
        mesh=mesh,
        in_specs=placed,
        out_specs=P(None, None, "shot", "rcv"),
        check_vma=False,
    )
```

time: 62.4 us -> 57.4 us (0.920)
  Pallas kernels: 58.7 us -> 55 us
  local copies, waits for them, and re-layouts: 3.56 us -> 2.3 us
    pallas_call x1, Pallas kernels: 58.7 us -> 55 us  [per_device(): pl.pallas_call(kernel, out_shape=jax.ShapeDtypeStruct((ROWS, rcv_here), B...]
    unnamed x10 -> x1, local copies, waits for them, and re-layouts: 3.56 us -> 2.3 us
where the time goes in v1:
time: 57.4 us; the launch traced here: 57.3 us
  Pallas kernels  55 us (96%)
  local copies, waits for them, and re-layouts  2.3 us (4%)
    pallas_call x1, Pallas kernels, per_device(): pl.pallas_call(kernel, out_shape=jax.ShapeDtypeStruct((ROWS, rcv_here), B...  55 us
    unnamed x1, local copies, waits for them, and re-layouts  2.3 us

profile of v1, /device:TPU:1, one launch (start us, length us, event | category | flops | bytes accessed | tf_op | source)
XLA Modules:
  0.0 57.3 jit_solution(2011935701229204128)
XLA Ops:
  0.0 55.0 %shard_map.46 = bf16[256,2048]{1,0:T(8,128)(2,1)} custom-call(bf16[256,2048]{1,0:T(8,128)(2,1)} %bitcast.4, s32[2,128]{1,0:T(2,128)} %bitcast.5, s32[4]{0:T(128)} %owner_hbm.1, s32[4,128]{1,0:T(4,128)} %recv_hbm.1), custom_call_target="tpu_custom_call" | custom-call | flops 2000000000 | bytes 2097152 | tf_op jit(solution)/shard_map/pallas_call | solution.py:239
  55.0 2.3 %copy.6 = bf16[1,2,128,2048]{3,2,1,0:T(8,128)(2,1)} copy(bf16[1,2,128,2048]{3,2,1,0:T(8,128)(2,1)} %bitcast.3) | data formatting | bytes 2097152

commit v2 on v1

--- a/solution.py
+++ b/solution.py
@@ -69,6 +69,8 @@
         pl.semaphore_signal(barrier, inc=1, device_id=line(d)[1], device_id_type=MESH)
     pl.semaphore_signal(barrier, inc=1, device_id=other_core, device_id_type=MESH)
     pl.semaphore_signal(barrier, inc=1, device_id=other_x, device_id_type=MESH)
+    for copy in inputs:
+        copy.wait()
     pl.semaphore_wait(barrier, 3 * (NQ - 1) + NZ - 1 + 2)
 
     def columns(index, n):
@@ -77,7 +79,7 @@
     def s1(n, e, d, source):
         index = lax.rem(q + d, NQ)
         return remote(
-            rec_hbm.at[pl.ds(e * BLOCK, BLOCK), columns(index, n)], scat[n].at[e, source],
+            rec.at[pl.ds(e * BLOCK, BLOCK), columns(index, n)], scat[n].at[e, source],
             s1s.at[n, e, d], s1r.at[n, e, source], at(index, lax.rem(z + e * SHIFT[n], NZ)),
         )
 
@@ -92,6 +94,9 @@
         index, device = plane(d)
         return remote(stage.at[n, index], out.at[:, columns(source, n)], os.at[n, d], orr.at[n, source], device)
 
+    def own(n):
+        return pltpu.make_async_copy(stage.at[n, q], out.at[:, columns(q, n)], ins.at[len(inputs) + n])
+
     def n2(d, source):
         return remote(near.at[q, core], near.at[source, core], n2s.at[d], n2r.at[source], plane(d)[1])
 
@@ -99,14 +104,11 @@
         return remote(near.at[index, half], near.at[index, half], n3s.at[index], n3r.at[index], other_core)
 
     offsets = [[(e, d) for d in range(NQ) for e in (1, 0) if (e, d) != (0, 0)]] * NC
-    for n in range(NC):
+    def scatter(n):
         for e, d in offsets[n]:
             s1(n, e, d, q).start()
-    for copy in inputs:
-        copy.wait()
-    for n in range(NC):
-        scat[n][0, q] = rec[:BLOCK, columns(q, n)]
-
+
+    scatter(0)
     first = r * (NQ * SHARE)
     points = jnp.concatenate([receivers[b : b + 1, :] for b in range(NBLK)], axis=1)
     tile = 256
@@ -134,12 +136,15 @@
 
     n1a = remote(local.at[1 - core], given.at[0], n1s.at[0], n1r.at[0], other_core)
     n1a.start()
+    for n in range(NC):
+        scat[n][0, q] = rec[:BLOCK, columns(q, n)]
     tail = jnp.concatenate([apertures[a : a + 1] for a in range(APER)], axis=1)
     near[q, core, BLOCK:] = jnp.broadcast_to(tail, (TAIL, WIDTH)).astype(BF16)
     n1a.wait_recv()
     given[2] = local[core] + given[0]
     n1b = remote(given.at[2], given.at[1], n1s.at[1], n1r.at[1], other_x)
     n1b.start()
+    scatter(1)
 
     zb = [owner[b] // NQ for b in range(NBLK)]
     qb = [lax.rem(owner[b], NQ) for b in range(NBLK)]
@@ -173,11 +178,11 @@
     n3(q, core).start()
     to_line(1)
     gather_line(0)
-    gather_line(1)
     for d in range(1, NQ):
         source = lax.rem(q + d, NQ)
         n2(d, source).wait_recv()
         n3(source, core).start()
+    gather_line(1)
     for d in range(NQ):
         index = lax.rem(q + d, NQ)
         n3(index, 1 - core).wait_recv()
@@ -190,6 +195,16 @@
                     near[index, c, :BLOCK, :BLOCK] * use[0] + near[index, c, :BLOCK, BLOCK:] * use[1]
                 )
 
+    n1a.wait_send()
+    n1b.wait_send()
+    for d in range(1, NQ):
+        n2(d, q).wait_send()
+    for n in range(NC):
+        for e, d in offsets[n]:
+            s1(n, e, d, q).wait_send()
+        for d in range(1, NZ):
+            s2(n, d, z).wait_send()
+
     factor = (2.0 * APER * BLOCK) ** (-0.5)
     for n in range(NC):
         for d in range(1, NZ):
@@ -197,39 +212,37 @@
         for k in range(NZ):
             for b in range(NBLK):
                 for c in range(2):
-                    far[n, c, b * BLOCK + k * SUB : b * BLOCK + (k + 1) * SUB] = gath[n, k, b, c]
+                    start = b * BLOCK + k * SUB
+                    far[n, start : start + SUB, c * LANES : (c + 1) * LANES] = gath[n, k, b, c]
 
         def product(index):
             rows = lhs[index].reshape(ROWS, NBLK * BLOCK)
-            by_real = jnp.dot(rows, far[n, 0], preferred_element_type=F32)
-            by_imag = jnp.dot(rows, far[n, 1], preferred_element_type=F32)
-            real = by_real[:BLOCK] - by_imag[BLOCK:]
-            imag = by_real[BLOCK:] + by_imag[:BLOCK]
+            both = jnp.dot(rows, far[n], preferred_element_type=F32)
+            real = both[:BLOCK, :LANES] - both[BLOCK:, LANES:]
+            imag = both[BLOCK:, :LANES] + both[:BLOCK, LANES:]
             return (jnp.concatenate([real, imag], axis=0) * factor).astype(BF16)
 
         for d in range(1, NQ):
             index = lax.rem(q + d, NQ)
             stage[n, index] = product(index)
             o(n, d, q).start()
-        out[:, columns(q, n)] = product(q)
+        stage[n, q] = product(q)
+        own(n).start()
+        for d in range(1, NZ):
+            s3(n, d, z).wait_send()
+        if n == 0:
+            for index in range(NQ):
+                n3(index, core).wait_send()
+        else:
+            for d in range(1, NQ):
+                o(n - 1, d, q).wait_send()
 
     for n in range(NC):
+        own(n).wait()
         for d in range(1, NQ):
             o(n, d, lax.rem(q + d, NQ)).wait_recv()
-    n1a.wait_send()
-    n1b.wait_send()
-    for d in range(1, NQ):
-        n2(d, q).wait_send()
-    for index in range(NQ):
-        n3(index, core).wait_send()
-    for n in range(NC):
-        for e, d in offsets[n]:
-            s1(n, e, d, q).wait_send()
-        for d in range(1, NQ):
-            o(n, d, q).wait_send()
-        for d in range(1, NZ):
-            s2(n, d, z).wait_send()
-            s3(n, d, z).wait_send()
+    for d in range(1, NQ):
+        o(NC - 1, d, q).wait_send()
 
 
 def per_device(records, aperture, block_owner, block_receivers):
@@ -240,7 +253,7 @@
         kernel,
         out_shape=jax.ShapeDtypeStruct((ROWS, rcv_here), BF16),
         in_specs=[hbm] * 4,
-        out_specs=pl.BlockSpec(memory_space=pltpu.VMEM),
+        out_specs=hbm,
         scratch_shapes=[
             pltpu.VMEM((ROWS, NQ * SHARE), BF16),
             pltpu.VMEM((APER, BLOCK), jnp.int32),
@@ -253,13 +266,13 @@
             pltpu.VMEM((NC, NZ, NBLK, SUB, LANES), BF16),
             pltpu.VMEM((NC, NBLK, 2, SUB, LANES), BF16),
             pltpu.VMEM((NC, NZ, NBLK, 2, SUB, LANES), BF16),
-            pltpu.VMEM((NC, 2, NBLK * BLOCK, LANES), BF16),
+            pltpu.VMEM((NC, NBLK * BLOCK, 2 * LANES), BF16),
             pltpu.VMEM((NQ, 2, BLOCK + TAIL, WIDTH), BF16),
             pltpu.VMEM((2, BLOCK, WIDTH), BF16),
             pltpu.VMEM((3, BLOCK, WIDTH), BF16),
             pltpu.VMEM((NQ, 2, BLOCK, NBLK * BLOCK), BF16),
             pltpu.VMEM((NC, NQ, ROWS, LANES), BF16),
-            dma((4,)),
+            dma((4 + NC,)),
             dma((NC, 2, NQ)), dma((NC, 2, NQ)),
             dma((NC, NZ)), dma((NC, NZ)),
             dma((NC, NZ)), dma((NC, NZ)),

time: 57.4 us -> 54 us (0.941)
  Pallas kernels: 55 us -> 51.6 us
    pallas_call x1, Pallas kernels: 55 us -> 51.6 us  [per_device(): pl.pallas_call(kernel, out_shape=jax.ShapeDtypeStruct((ROWS, rcv_here), B...]
where the time goes in v2:
time: 54 us; the launch traced here: 53.9 us
  Pallas kernels  51.6 us (96%)
  local copies, waits for them, and re-layouts  2.3 us (4%)
    pallas_call x1, Pallas kernels, per_device(): pl.pallas_call(kernel, out_shape=jax.ShapeDtypeStruct((ROWS, rcv_here), B...  51.6 us
    unnamed x1, local copies, waits for them, and re-layouts  2.3 us

profile of v2, /device:TPU:1, one launch (start us, length us, event | category | flops | bytes accessed | tf_op | source)
XLA Modules:
  0.0 53.9 jit_solution(9833460514795802245)
XLA Ops:
  0.0 51.6 %shard_map.46 = bf16[256,2048]{1,0:T(8,128)(2,1)} custom-call(bf16[256,2048]{1,0:T(8,128)(2,1)} %bitcast.4, s32[2,128]{1,0:T(2,128)} %bitcast.5, s32[4]{0:T(128)} %owner_hbm.1, s32[4,128]{1,0:T(4,128)} %recv_hbm.1), custom_call_target="tpu_custom_call" | custom-call | flops 2000000000 | bytes 2097152 | tf_op jit(solution)/shard_map/pallas_call | solution.py:252
  51.6 2.3 %copy.6 = bf16[1,2,128,2048]{3,2,1,0:T(8,128)(2,1)} copy(bf16[1,2,128,2048]{3,2,1,0:T(8,128)(2,1)} %bitcast.3) | data formatting | bytes 2097152

commit v3 on v2

--- a/solution.py
+++ b/solution.py
@@ -20,6 +20,8 @@
 SUB = BLOCK // NZ
 WIDTH = APER * BLOCK
 TAIL = 16
+FAR_FIRST = ((0, 0), (1, 2), (1, 1), (1, 3), (0, 2), (1, 0), (0, 1), (0, 3))
+LINE = (4, 3, 5, 2, 6, 1, 7)
 SHIFT = (1, NZ - 1)
 
 
@@ -52,9 +54,12 @@
     def at(index, plane):
         return (plane * NQ + index, r)
 
+    def beside(d):
+        dx, dy = FAR_FIRST[d]
+        return lax.rem(q // NY + dx, NX) * NY + lax.rem(q + dy, NY)
+
     def plane(d):
-        index = lax.rem(q + d, NQ)
-        return index, at(index, z)
+        return beside(d), at(beside(d), z)
 
     def line(d):
         index = lax.rem(z + d, NZ)
@@ -62,10 +67,10 @@
 
     barrier = pltpu.get_barrier_semaphore()
     for d in range(1, NQ):
-        index = lax.rem(q + d, NQ)
+        index = beside(d)
         for plane_of in (z, *(lax.rem(z + shift, NZ) for shift in SHIFT)):
             pl.semaphore_signal(barrier, inc=1, device_id=at(index, plane_of), device_id_type=MESH)
-    for d in range(1, NZ):
+    for d in LINE:
         pl.semaphore_signal(barrier, inc=1, device_id=line(d)[1], device_id_type=MESH)
     pl.semaphore_signal(barrier, inc=1, device_id=other_core, device_id_type=MESH)
     pl.semaphore_signal(barrier, inc=1, device_id=other_x, device_id_type=MESH)
@@ -77,7 +82,7 @@
         return pl.ds(pl.multiple_of(index * SHARE + n * LANES, LANES), LANES)
 
     def s1(n, e, d, source):
-        index = lax.rem(q + d, NQ)
+        index = beside(d)
         return remote(
             rec.at[pl.ds(e * BLOCK, BLOCK), columns(index, n)], scat[n].at[e, source],
             s1s.at[n, e, d], s1r.at[n, e, source], at(index, lax.rem(z + e * SHIFT[n], NZ)),
@@ -151,22 +156,22 @@
 
     def to_line(n):
         for e, d in offsets[n]:
-            s1(n, e, d, lax.rem(q + d, NQ)).wait_recv()
+            s1(n, e, d, beside(d)).wait_recv()
         for b in range(NBLK):
             piece = scat[n][jnp.where(zb[b] == z, 0, 1), qb[b]]
             for k in range(NZ):
                 sel[n, k, b] = piece[k * SUB : (k + 1) * SUB]
-        for d in range(1, NZ):
+        for d in LINE:
             s2(n, d, z).start()
         zscat[n][z] = sel[n, z]
 
     def gather_line(n):
-        for d in range(1, NZ):
+        for d in LINE:
             s2(n, d, lax.rem(z + d, NZ)).wait_recv()
         for b in range(NBLK):
             for c in range(2):
                 part[n, b, c] = zscat[n][lax.rem(zb[b] + c * SHIFT[n], NZ), b]
-        for d in range(1, NZ):
+        for d in LINE:
             s3(n, d, z).start()
         gath[n, z] = part[n]
 
@@ -179,12 +184,12 @@
     to_line(1)
     gather_line(0)
     for d in range(1, NQ):
-        source = lax.rem(q + d, NQ)
+        source = beside(d)
         n2(d, source).wait_recv()
         n3(source, core).start()
     gather_line(1)
     for d in range(NQ):
-        index = lax.rem(q + d, NQ)
+        index = beside(d)
         n3(index, 1 - core).wait_recv()
         tail = near[index, 0, BLOCK:].astype(F32)
         blocks = [upright(tail[:1, a * BLOCK : (a + 1) * BLOCK]) for a in range(APER)]
@@ -202,12 +207,12 @@
     for n in range(NC):
         for e, d in offsets[n]:
             s1(n, e, d, q).wait_send()
-        for d in range(1, NZ):
+        for d in LINE:
             s2(n, d, z).wait_send()
 
     factor = (2.0 * APER * BLOCK) ** (-0.5)
     for n in range(NC):
-        for d in range(1, NZ):
+        for d in LINE:
             s3(n, d, lax.rem(z + d, NZ)).wait_recv()
         for k in range(NZ):
             for b in range(NBLK):
@@ -223,12 +228,12 @@
             return (jnp.concatenate([real, imag], axis=0) * factor).astype(BF16)
 
         for d in range(1, NQ):
-            index = lax.rem(q + d, NQ)
+            index = beside(d)
             stage[n, index] = product(index)
             o(n, d, q).start()
         stage[n, q] = product(q)
         own(n).start()
-        for d in range(1, NZ):
+        for d in LINE:
             s3(n, d, z).wait_send()
         if n == 0:
             for index in range(NQ):
@@ -240,7 +245,7 @@
     for n in range(NC):
         own(n).wait()
         for d in range(1, NQ):
-            o(n, d, lax.rem(q + d, NQ)).wait_recv()
+            o(n, d, beside(d)).wait_recv()
     for d in range(1, NQ):
         o(NC - 1, d, q).wait_send()
 

time: 54 us -> 52 us (0.963); the launches traced: 53.9 us -> 51.1 us
  Pallas kernels: 51.6 us -> 48.8 us
    pallas_call x1, Pallas kernels: 51.6 us -> 48.8 us  [per_device(): pl.pallas_call(kernel, out_shape=jax.ShapeDtypeStruct((ROWS, rcv_here), B...]
where the time goes in v3:
time: 52 us; the launch traced here: 51.1 us
  Pallas kernels  48.8 us (94%)
  local copies, waits for them, and re-layouts  2.3 us (4%)
    pallas_call x1, Pallas kernels, per_device(): pl.pallas_call(kernel, out_shape=jax.ShapeDtypeStruct((ROWS, rcv_here), B...  48.8 us
    unnamed x1, local copies, waits for them, and re-layouts  2.3 us

profile of v3, /device:TPU:1, one launch (start us, length us, event | category | flops | bytes accessed | tf_op | source)
XLA Modules:
  0.0 51.1 jit_solution(16820534581680436875)
XLA Ops:
  0.0 48.8 %shard_map.46 = bf16[256,2048]{1,0:T(8,128)(2,1)} custom-call(bf16[256,2048]{1,0:T(8,128)(2,1)} %bitcast.4, s32[2,128]{1,0:T(2,128)} %bitcast.5, s32[4]{0:T(128)} %owner_hbm.1, s32[4,128]{1,0:T(4,128)} %recv_hbm.1), custom_call_target="tpu_custom_call" | custom-call | flops 2000000000 | bytes 2097152 | tf_op jit(solution)/shard_map/pallas_call | solution.py:257
  48.8 2.3 %copy.6 = bf16[1,2,128,2048]{3,2,1,0:T(8,128)(2,1)} copy(bf16[1,2,128,2048]{3,2,1,0:T(8,128)(2,1)} %bitcast.3) | data formatting | bytes 2097152

commit v4 on v3

--- a/solution.py
+++ b/solution.py
@@ -66,12 +66,11 @@
         return index, at(q, index)
 
     barrier = pltpu.get_barrier_semaphore()
-    for d in range(1, NQ):
-        index = beside(d)
-        for plane_of in (z, *(lax.rem(z + shift, NZ) for shift in SHIFT)):
-            pl.semaphore_signal(barrier, inc=1, device_id=at(index, plane_of), device_id_type=MESH)
-    for d in LINE:
-        pl.semaphore_signal(barrier, inc=1, device_id=line(d)[1], device_id_type=MESH)
+    steps = [(d, shift) for d in range(1, NQ) for shift in (0, *SHIFT)] + [(0, shift) for shift in LINE]
+    hops = {d: dx + min(dy, NY - dy) for d, (dx, dy) in enumerate(FAR_FIRST)}
+    for d, shift in sorted(steps, key=lambda step: -(hops[step[0]] + min(step[1], NZ - step[1]))):
+        device = at(beside(d), lax.rem(z + shift, NZ))
+        pl.semaphore_signal(barrier, inc=1, device_id=device, device_id_type=MESH)
     pl.semaphore_signal(barrier, inc=1, device_id=other_core, device_id_type=MESH)
     pl.semaphore_signal(barrier, inc=1, device_id=other_x, device_id_type=MESH)
     for copy in inputs:

time: 52 us -> 52 us (level)
  no operation moved by 1% of the time
where the time goes in v4:
time: 52 us; the launch traced here: 51 us
  Pallas kernels  48.7 us (94%)
  local copies, waits for them, and re-layouts  2.3 us (4%)
    pallas_call x1, Pallas kernels, per_device(): pl.pallas_call(kernel, out_shape=jax.ShapeDtypeStruct((ROWS, rcv_here), B...  48.7 us
    unnamed x1, local copies, waits for them, and re-layouts  2.3 us

profile of v4, /device:TPU:1, one launch (start us, length us, event | category | flops | bytes accessed | tf_op | source)
XLA Modules:
  0.0 51.0 jit_solution(13095803271119252996)
XLA Ops:
  0.0 48.7 %shard_map.46 = bf16[256,2048]{1,0:T(8,128)(2,1)} custom-call(bf16[256,2048]{1,0:T(8,128)(2,1)} %bitcast.4, s32[2,128]{1,0:T(2,128)} %bitcast.5, s32[4]{0:T(128)} %owner_hbm.1, s32[4,128]{1,0:T(4,128)} %recv_hbm.1), custom_call_target="tpu_custom_call" | custom-call | flops 2000000000 | bytes 2097152 | tf_op jit(solution)/shard_map/pallas_call | solution.py:256
  48.7 2.3 %copy.6 = bf16[1,2,128,2048]{3,2,1,0:T(8,128)(2,1)} copy(bf16[1,2,128,2048]{3,2,1,0:T(8,128)(2,1)} %bitcast.3) | data formatting | bytes 2097152
